TPU v7x, 128 devices: a whole 4x4x4 slice. The times are simulated.
128 devices in a mesh: grp: 4 (over x), sta: 32 (over z, y, core).
Axes of the slice: x: 4, y: 4, z: 4, core: 2. Of those that a mesh axis runs over, the one named last changes fastest.
Arguments:
- spectra: float32 [1024, 2, 18432], P(('grp', 'sta')), may hold values from -61 to 61
- stacks: float32 [12288, 1601], P(('grp', 'sta')), may hold values from -6 to 6
- pair_sta: int32 [2, 12288], P(None, ('grp', 'sta')), may hold values from 0 to 255
- pair_valid: int32 [12288], P(('grp', 'sta')), may hold values 0 or 1
- owner: int32 [12288, 1], P(('grp', 'sta')), may hold values from 0 to 127; in each aligned block of 96 rows (0 to 95, 96 to 191, ...) at most 2 rows name the same one
- slot: int32 [12288], P(('grp', 'sta')), may hold values from 0 to 95
Outputs:
- stacks_new: float32 [12288, 1601], P(('grp', 'sta'))
Inputs may be any that keep to these rules, and one draw needn't show every extreme that they name: Among the 96 rows of one device no owner is named more than 2 times.
All inputs are finite; a program needn't handle non-finite values. No bound on the sum of `pair_valid` on one device may be relied on, other than what follows from the above.
Results may differ from a plain program's by a relative error of at most 0.0041.
Values may be sent and summed in bfloat16 or wider, within the bound.
A program may use at most 128 MiB of HBM per device.

v0:
```python
import math
import jax
import jax.numpy as jnp
from jax import lax
from jax.sharding import PartitionSpec as P

BAND = 64


def cut_along(x, dim, length):
    shape = x.shape
    tiles = x.reshape(*shape[:dim], length, shape[dim] // length, *shape[dim + 1 :])
    return jnp.moveaxis(tiles, dim, 0)


def joined_along(tiles, dim):
    shape = list(tiles.shape[1:])
    shape[dim] *= tiles.shape[0]
    return jnp.moveaxis(tiles, 0, dim).reshape(shape)


def joined_exchange(x, axis, axes, splits, concats):
    sizes = [lax.axis_size(a) for a in axes]
    tiles = cut_along(x, splits[0], sizes[0])
    tiles = jnp.moveaxis(cut_along(tiles, splits[1] + 1, sizes[1]), 0, 1)
    inside = tiles.shape[2:]
    tiles = tiles.reshape(-1, *inside)
    tiles = lax.all_to_all(tiles, axis, split_axis=0, concat_axis=0, tiled=True)
    tiles = joined_along(tiles.reshape(*sizes, *inside), concats[0] + 1)
    return joined_along(tiles, concats[1])


def whiten(spectra):
    shape = spectra.shape
    split = spectra.reshape(shape[0], 2, shape[2] // BAND, BAND)
    power = jnp.mean(split * split, axis=(1, 3), keepdims=True)
    return (split * lax.rsqrt(power + 1e-06)).reshape(shape).astype(jnp.bfloat16)


def table_block(start, width, lag_count, total_bins):
    freqs = start + lax.iota(jnp.int32, width)
    shifts = lax.iota(jnp.int32, lag_count) - (lag_count - 1) // 2
    angle_ids = jnp.mod(freqs[:, None] * shifts[None, :], 2 * total_bins)
    theta = angle_ids.astype(jnp.float32) * jnp.float32(math.pi / total_bins)
    return (jnp.cos(theta).astype(jnp.bfloat16), (-jnp.sin(theta)).astype(jnp.bfloat16))


def local(spectra, stacks, pair_sta, pair_valid, owner, slot):
    total_bins = spectra.shape[2]
    lag_count = stacks.shape[1]
    stack_rows = stacks.shape[0]
    pair_count = pair_sta.shape[1]
    groups = lax.axis_size("grp")
    members = lax.axis_size("sta")
    devices = groups * members
    capacity = max(2, (4 * pair_count + 3 * devices - 1) // (3 * devices))
    whitened = whiten(spectra)
    gathered = lax.all_gather(whitened, "sta", axis=0, tiled=True)
    first = jnp.take(gathered, pair_sta[0], axis=0)
    second = jnp.take(gathered, pair_sta[1], axis=0)
    fblock = 2048

    def add_block(index, total):
        start = index * fblock
        left = lax.dynamic_slice_in_dim(first, start, fblock, 2).astype(jnp.float32)
        right = lax.dynamic_slice_in_dim(second, start, fblock, 2).astype(jnp.float32)
        real_part = (left[:, 0] * right[:, 0] + left[:, 1] * right[:, 1]).astype(jnp.bfloat16)
        imag_part = (left[:, 1] * right[:, 0] - left[:, 0] * right[:, 1]).astype(jnp.bfloat16)
        cosines, sines = table_block(start, fblock, lag_count, total_bins)
        total = total + jnp.dot(real_part, cosines, preferred_element_type=jnp.float32)
        return total + jnp.dot(imag_part, sines, preferred_element_type=jnp.float32)

    corr = lax.fori_loop(
        0, total_bins // fblock, add_block, jnp.zeros((pair_count, lag_count), jnp.float32)
    )
    corr = corr * jnp.float32(total_bins ** (-0.5)) * pair_valid.astype(jnp.float32)[:, None]
    dest = owner[:, 0]
    dest_hot = (dest[:, None] == lax.iota(jnp.int32, devices)[None, :]).astype(jnp.int32)
    before = jnp.cumsum(dest_hot, axis=0) - dest_hot
    position = jnp.sum(before * dest_hot, axis=1)
    flat = dest * capacity + position
    placing = (flat[:, None] == lax.iota(jnp.int32, devices * capacity)[None, :]).astype(
        jnp.float32
    )
    send_rows = jnp.dot(placing.T, corr, precision=lax.Precision.HIGHEST)
    send_slots = jnp.dot(
        placing.T, slot.astype(jnp.float32)[:, None], precision=lax.Precision.HIGHEST
    )[:, 0]
    got_rows, got_slots = (
        joined_exchange(
            send_rows.reshape(groups, members, capacity, lag_count),
            ("grp", "sta"),
            ("grp", "sta"),
            (0, 1),
            (0, 1),
        ),
        joined_exchange(
            send_slots.reshape(groups, members, capacity),
            ("grp", "sta"),
            ("grp", "sta"),
            (0, 1),
            (0, 1),
        ),
    )
    got_rows = got_rows.reshape(devices * capacity, lag_count)
    got_slots = got_slots.reshape(devices * capacity)
    adding = (
        got_slots[None, :] == lax.iota(jnp.int32, stack_rows).astype(jnp.float32)[:, None]
    ).astype(jnp.float32)
    return stacks + jnp.dot(adding, got_rows, precision=lax.Precision.HIGHEST)


def solution(mesh):
    return jax.shard_map(
        local,
        mesh=mesh,
        in_specs=(
            P(("grp", "sta"), None, None),
            P(("grp", "sta"), None),
            P(None, ("grp", "sta")),
            P(("grp", "sta")),
            P(("grp", "sta"), None),
            P(("grp", "sta")),
        ),
        out_specs=P(("grp", "sta"), None),
        check_vma=False,
    )
```

profile of v0, /device:TPU:1, one launch (start us, length us, event | category | flops | bytes accessed | tf_op | source)
XLA Modules:
  0.0 1220.7 jit_solution(18075538447004292541)
XLA Ops:
  6.6 2.9 multiply_reduce_fusion
  9.5 0.5 reduce_sum.30
  10.0 0.5 reduce_sum.31
  10.5 0.4 mul.157
  10.8 0.4 mul.158
  11.2 1.4 multiply_convert_fusion
  13.1 1.0 fusion.22
  14.1 11.5 all-to-all-start
  25.7 68.5 %all-gather.2.cloned.1.call-done = bf16[256,2,18432]{2,1,0:T(2,128)(2,1)} async-done(((bf16[8,2,18432]{2,1,0:T(2,128)(2,1)}), bf16[256,2,18432]{2,1,0:T(2,128)(2,1)}) %all-gather.2.cloned.1.call-update) | async-done | bytes 18874384 | tf_op jit(solution)/shard_map/all_gather | solution.py:58
  94.3 23.4 %gather_fusion = bf16[96,2,18432]{2,1,0:T(2,128)(2,1)} fusion(bf16[256,2,18432]{2,1,0:T(2,128)(2,1)} %all-gather.2.cloned.1.call-done, s32[1024]{0:T(1024)S(1)} %pad_clamp_fusion.1), kind=kCustom, calls=%fused_computation.clone | custom fusion | bytes 14156160 | tf_op jit(solution)/shard_map/jit(_take)/gather | solution.py:59
  117.6 23.3 %gather_fusion.1 = bf16[96,2,18432]{2,1,0:T(2,128)(2,1)} fusion(bf16[256,2,18432]{2,1,0:T(2,128)(2,1)} %all-gather.2.cloned.1.call-done, s32[1024]{0:T(1024)S(1)} %pad_clamp_fusion), kind=kCustom, calls=%fused_computation.1.clone | custom fusion | bytes 14156160 | tf_op jit(solution)/shard_map/jit(_take)/gather | solution.py:60
  140.9 16.3 %broadcast_select_fusion = (bf16[96,2,18432]{2,1,0:T(2,128)(2,1)}, bf16[96,2,18432]{2,1,0:T(2,128)(2,1)}) fusion(bf16[96,2,18432]{2,1,0:T(2,128)(2,1)} %gather_fusion.1, pred[96]{0:T(512)(128)(4,1)S(1)} %get-tuple-element.150, bf16[96,2,18432]{2,1,0:T(2,128)(2,1)} %gather_fusion, pred[96]{0:T(512)(128)(4,1)S(1)} %get-tuple-element.156), kind=kLoop, calls=%fused_computation.31 | loop fusion | flops 7077888 | bytes 28311744 | tf_op jit(solution)/shard_map/jit(_take)/select_n | solution.py:60
  157.2 1014.8 %while.16 = (s32[]{:T(128)}, f32[96,1601]{1,0:T(8,128)}, bf16[96,2,18432]{2,1,0:T(2,128)(2,1)}, bf16[96,2,18432]{2,1,0:T(2,128)(2,1)}, s32[]{:T(128)}, /*index=5*/s32[]{:T(128)}, s32[]{:T(128)}, s32[]{:T(128)}) while((s32[]{:T(128)}, f32[96,1601]{1,0:T(8,128)}, bf16[96,2,18432]{2,1,0:T(2,128)(2,1)}, ...), condition=%wide.region_5.7_spmd.clone, body=%wide.region_4.6_spmd.clone.sunk | while | flops 1330757632 | bytes 16658849 | solution.py:73
  177.0 2.5 constant_dynamic-slice_fusion.3
  179.4 0.3 copy_convert_fusion.4
  179.7 0.3 copy_convert_fusion.5
  180.0 52.4 %fusion.42 = f32[96,1601]{1,0:T(8,128)S(1)} fusion(s32[1601]{0:T(1024)S(1)} %iota_add_fusion.4, s32[2048]{0:T(1024)S(1)} %iota_add_fusion.5, f32[96,1601]{1,0:T(8,128)} %get-tuple-element.198, f32[96,2,2048]{2,0,1:T(8,128)S(1)} %copy_convert_fusion.4, f32[96,2,2048]{2,0,1:T(8,128)S(1)} %copy_convert_fusion.5, pred[]{:T(512)S(6)} %compare.3), kind=kOutput, calls=%fused_computation.14.clone.3 | convolution fusion | flops 663421184 | bytes 4389893 | tf_op jit(solution)/shard_map/while/body/eval_jaxpr/dot_general | solution.py:70
  232.5 54.1 %fusion.43 = f32[96,1601]{1,0:T(8,128)} fusion(f32[96,1601]{1,0:T(8,128)S(1)} %fusion.42, s32[1601]{0:T(1024)S(1)} %iota_add_fusion.4, s32[2048]{0:T(1024)S(1)} %iota_add_fusion.5, f32[96,2,2048]{2,0,1:T(8,128)S(1)} %copy_convert_fusion.4, f32[96,2,2048]{2,0,1:T(8,128)S(1)} %copy_convert_fusion.5), kind=kOutput, calls=%fused_computation.13.clone.3 | convolution fusion | flops 666546304 | bytes 4389892 | tf_op jit(solution)/shard_map/while/body/eval_jaxpr/dot_general | solution.py:71
  286.6 2.5 constant_dynamic-slice_fusion.3
  289.0 0.3 copy_convert_fusion.4
  289.3 0.3 copy_convert_fusion.5
  289.6 53.5 %fusion.42 = f32[96,1601]{1,0:T(8,128)S(1)} fusion(s32[1601]{0:T(1024)S(1)} %iota_add_fusion.4, s32[2048]{0:T(1024)S(1)} %iota_add_fusion.5, f32[96,1601]{1,0:T(8,128)} %get-tuple-element.198, f32[96,2,2048]{2,0,1:T(8,128)S(1)} %copy_convert_fusion.4, f32[96,2,2048]{2,0,1:T(8,128)S(1)} %copy_convert_fusion.5, pred[]{:T(512)S(6)} %compare.3), kind=kOutput, calls=%fused_computation.14.clone.3 | convolution fusion | flops 663421184 | bytes 4389893 | tf_op jit(solution)/shard_map/while/body/eval_jaxpr/dot_general | solution.py:70
  343.1 54.1 %fusion.43 = f32[96,1601]{1,0:T(8,128)} fusion(f32[96,1601]{1,0:T(8,128)S(1)} %fusion.42, s32[1601]{0:T(1024)S(1)} %iota_add_fusion.4, s32[2048]{0:T(1024)S(1)} %iota_add_fusion.5, f32[96,2,2048]{2,0,1:T(8,128)S(1)} %copy_convert_fusion.4, f32[96,2,2048]{2,0,1:T(8,128)S(1)} %copy_convert_fusion.5), kind=kOutput, calls=%fused_computation.13.clone.3 | convolution fusion | flops 666546304 | bytes 4389892 | tf_op jit(solution)/shard_map/while/body/eval_jaxpr/dot_general | solution.py:71
  397.2 2.5 constant_dynamic-slice_fusion.3
  399.7 0.3 copy_convert_fusion.4
  399.9 0.3 copy_convert_fusion.5
  400.3 53.5 %fusion.42 = f32[96,1601]{1,0:T(8,128)S(1)} fusion(s32[1601]{0:T(1024)S(1)} %iota_add_fusion.4, s32[2048]{0:T(1024)S(1)} %iota_add_fusion.5, f32[96,1601]{1,0:T(8,128)} %get-tuple-element.198, f32[96,2,2048]{2,0,1:T(8,128)S(1)} %copy_convert_fusion.4, f32[96,2,2048]{2,0,1:T(8,128)S(1)} %copy_convert_fusion.5, pred[]{:T(512)S(6)} %compare.3), kind=kOutput, calls=%fused_computation.14.clone.3 | convolution fusion | flops 663421184 | bytes 4389893 | tf_op jit(solution)/shard_map/while/body/eval_jaxpr/dot_general | solution.py:70
  453.8 54.1 %fusion.43 = f32[96,1601]{1,0:T(8,128)} fusion(f32[96,1601]{1,0:T(8,128)S(1)} %fusion.42, s32[1601]{0:T(1024)S(1)} %iota_add_fusion.4, s32[2048]{0:T(1024)S(1)} %iota_add_fusion.5, f32[96,2,2048]{2,0,1:T(8,128)S(1)} %copy_convert_fusion.4, f32[96,2,2048]{2,0,1:T(8,128)S(1)} %copy_convert_fusion.5), kind=kOutput, calls=%fused_computation.13.clone.3 | convolution fusion | flops 666546304 | bytes 4389892 | tf_op jit(solution)/shard_map/while/body/eval_jaxpr/dot_general | solution.py:71
  507.9 2.5 constant_dynamic-slice_fusion.3
  510.3 0.3 copy_convert_fusion.4
  510.6 0.3 copy_convert_fusion.5
  510.9 53.5 %fusion.42 = f32[96,1601]{1,0:T(8,128)S(1)} fusion(s32[1601]{0:T(1024)S(1)} %iota_add_fusion.4, s32[2048]{0:T(1024)S(1)} %iota_add_fusion.5, f32[96,1601]{1,0:T(8,128)} %get-tuple-element.198, f32[96,2,2048]{2,0,1:T(8,128)S(1)} %copy_convert_fusion.4, f32[96,2,2048]{2,0,1:T(8,128)S(1)} %copy_convert_fusion.5, pred[]{:T(512)S(6)} %compare.3), kind=kOutput, calls=%fused_computation.14.clone.3 | convolution fusion | flops 663421184 | bytes 4389893 | tf_op jit(solution)/shard_map/while/body/eval_jaxpr/dot_general | solution.py:70
  564.4 54.1 %fusion.43 = f32[96,1601]{1,0:T(8,128)} fusion(f32[96,1601]{1,0:T(8,128)S(1)} %fusion.42, s32[1601]{0:T(1024)S(1)} %iota_add_fusion.4, s32[2048]{0:T(1024)S(1)} %iota_add_fusion.5, f32[96,2,2048]{2,0,1:T(8,128)S(1)} %copy_convert_fusion.4, f32[96,2,2048]{2,0,1:T(8,128)S(1)} %copy_convert_fusion.5), kind=kOutput, calls=%fused_computation.13.clone.3 | convolution fusion | flops 666546304 | bytes 4389892 | tf_op jit(solution)/shard_map/while/body/eval_jaxpr/dot_general | solution.py:71
  618.5 2.5 constant_dynamic-slice_fusion.3
  621.0 0.3 copy_convert_fusion.4
  621.3 0.3 copy_convert_fusion.5
  621.6 53.5 %fusion.42 = f32[96,1601]{1,0:T(8,128)S(1)} fusion(s32[1601]{0:T(1024)S(1)} %iota_add_fusion.4, s32[2048]{0:T(1024)S(1)} %iota_add_fusion.5, f32[96,1601]{1,0:T(8,128)} %get-tuple-element.198, f32[96,2,2048]{2,0,1:T(8,128)S(1)} %copy_convert_fusion.4, f32[96,2,2048]{2,0,1:T(8,128)S(1)} %copy_convert_fusion.5, pred[]{:T(512)S(6)} %compare.3), kind=kOutput, calls=%fused_computation.14.clone.3 | convolution fusion | flops 663421184 | bytes 4389893 | tf_op jit(solution)/shard_map/while/body/eval_jaxpr/dot_general | solution.py:70
  675.1 54.1 %fusion.43 = f32[96,1601]{1,0:T(8,128)} fusion(f32[96,1601]{1,0:T(8,128)S(1)} %fusion.42, s32[1601]{0:T(1024)S(1)} %iota_add_fusion.4, s32[2048]{0:T(1024)S(1)} %iota_add_fusion.5, f32[96,2,2048]{2,0,1:T(8,128)S(1)} %copy_convert_fusion.4, f32[96,2,2048]{2,0,1:T(8,128)S(1)} %copy_convert_fusion.5), kind=kOutput, calls=%fused_computation.13.clone.3 | convolution fusion | flops 666546304 | bytes 4389892 | tf_op jit(solution)/shard_map/while/body/eval_jaxpr/dot_general | solution.py:71
  729.2 2.5 constant_dynamic-slice_fusion.3
  731.6 0.3 copy_convert_fusion.4
  731.9 0.3 copy_convert_fusion.5
  732.2 53.5 %fusion.42 = f32[96,1601]{1,0:T(8,128)S(1)} fusion(s32[1601]{0:T(1024)S(1)} %iota_add_fusion.4, s32[2048]{0:T(1024)S(1)} %iota_add_fusion.5, f32[96,1601]{1,0:T(8,128)} %get-tuple-element.198, f32[96,2,2048]{2,0,1:T(8,128)S(1)} %copy_convert_fusion.4, f32[96,2,2048]{2,0,1:T(8,128)S(1)} %copy_convert_fusion.5, pred[]{:T(512)S(6)} %compare.3), kind=kOutput, calls=%fused_computation.14.clone.3 | convolution fusion | flops 663421184 | bytes 4389893 | tf_op jit(solution)/shard_map/while/body/eval_jaxpr/dot_general | solution.py:70
  785.7 54.1 %fusion.43 = f32[96,1601]{1,0:T(8,128)} fusion(f32[96,1601]{1,0:T(8,128)S(1)} %fusion.42, s32[1601]{0:T(1024)S(1)} %iota_add_fusion.4, s32[2048]{0:T(1024)S(1)} %iota_add_fusion.5, f32[96,2,2048]{2,0,1:T(8,128)S(1)} %copy_convert_fusion.4, f32[96,2,2048]{2,0,1:T(8,128)S(1)} %copy_convert_fusion.5), kind=kOutput, calls=%fused_computation.13.clone.3 | convolution fusion | flops 666546304 | bytes 4389892 | tf_op jit(solution)/shard_map/while/body/eval_jaxpr/dot_general | solution.py:71
  839.8 2.5 constant_dynamic-slice_fusion.3
  842.3 0.3 copy_convert_fusion.4
  842.6 0.3 copy_convert_fusion.5
  842.9 53.5 %fusion.42 = f32[96,1601]{1,0:T(8,128)S(1)} fusion(s32[1601]{0:T(1024)S(1)} %iota_add_fusion.4, s32[2048]{0:T(1024)S(1)} %iota_add_fusion.5, f32[96,1601]{1,0:T(8,128)} %get-tuple-element.198, f32[96,2,2048]{2,0,1:T(8,128)S(1)} %copy_convert_fusion.4, f32[96,2,2048]{2,0,1:T(8,128)S(1)} %copy_convert_fusion.5, pred[]{:T(512)S(6)} %compare.3), kind=kOutput, calls=%fused_computation.14.clone.3 | convolution fusion | flops 663421184 | bytes 4389893 | tf_op jit(solution)/shard_map/while/body/eval_jaxpr/dot_general | solution.py:70
  896.4 54.1 %fusion.43 = f32[96,1601]{1,0:T(8,128)} fusion(f32[96,1601]{1,0:T(8,128)S(1)} %fusion.42, s32[1601]{0:T(1024)S(1)} %iota_add_fusion.4, s32[2048]{0:T(1024)S(1)} %iota_add_fusion.5, f32[96,2,2048]{2,0,1:T(8,128)S(1)} %copy_convert_fusion.4, f32[96,2,2048]{2,0,1:T(8,128)S(1)} %copy_convert_fusion.5), kind=kOutput, calls=%fused_computation.13.clone.3 | convolution fusion | flops 666546304 | bytes 4389892 | tf_op jit(solution)/shard_map/while/body/eval_jaxpr/dot_general | solution.py:71
  950.5 2.5 constant_dynamic-slice_fusion.3
  952.9 0.3 copy_convert_fusion.4
  953.2 0.3 copy_convert_fusion.5
  953.5 53.5 %fusion.42 = f32[96,1601]{1,0:T(8,128)S(1)} fusion(s32[1601]{0:T(1024)S(1)} %iota_add_fusion.4, s32[2048]{0:T(1024)S(1)} %iota_add_fusion.5, f32[96,1601]{1,0:T(8,128)} %get-tuple-element.198, f32[96,2,2048]{2,0,1:T(8,128)S(1)} %copy_convert_fusion.4, f32[96,2,2048]{2,0,1:T(8,128)S(1)} %copy_convert_fusion.5, pred[]{:T(512)S(6)} %compare.3), kind=kOutput, calls=%fused_computation.14.clone.3 | convolution fusion | flops 663421184 | bytes 4389893 | tf_op jit(solution)/shard_map/while/body/eval_jaxpr/dot_general | solution.py:70
  1007.0 54.1 %fusion.43 = f32[96,1601]{1,0:T(8,128)} fusion(f32[96,1601]{1,0:T(8,128)S(1)} %fusion.42, s32[1601]{0:T(1024)S(1)} %iota_add_fusion.4, s32[2048]{0:T(1024)S(1)} %iota_add_fusion.5, f32[96,2,2048]{2,0,1:T(8,128)S(1)} %copy_convert_fusion.4, f32[96,2,2048]{2,0,1:T(8,128)S(1)} %copy_convert_fusion.5), kind=kOutput, calls=%fused_computation.13.clone.3 | convolution fusion | flops 666546304 | bytes 4389892 | tf_op jit(solution)/shard_map/while/body/eval_jaxpr/dot_general | solution.py:71
  1061.1 2.5 constant_dynamic-slice_fusion.3
  1063.6 0.3 copy_convert_fusion.4
  1063.9 0.3 copy_convert_fusion.5
  1064.2 53.5 %fusion.42 = f32[96,1601]{1,0:T(8,128)S(1)} fusion(s32[1601]{0:T(1024)S(1)} %iota_add_fusion.4, s32[2048]{0:T(1024)S(1)} %iota_add_fusion.5, f32[96,1601]{1,0:T(8,128)} %get-tuple-element.198, f32[96,2,2048]{2,0,1:T(8,128)S(1)} %copy_convert_fusion.4, f32[96,2,2048]{2,0,1:T(8,128)S(1)} %copy_convert_fusion.5, pred[]{:T(512)S(6)} %compare.3), kind=kOutput, calls=%fused_computation.14.clone.3 | convolution fusion | flops 663421184 | bytes 4389893 | tf_op jit(solution)/shard_map/while/body/eval_jaxpr/dot_general | solution.py:70
  1117.7 54.1 %fusion.43 = f32[96,1601]{1,0:T(8,128)} fusion(f32[96,1601]{1,0:T(8,128)S(1)} %fusion.42, s32[1601]{0:T(1024)S(1)} %iota_add_fusion.4, s32[2048]{0:T(1024)S(1)} %iota_add_fusion.5, f32[96,2,2048]{2,0,1:T(8,128)S(1)} %copy_convert_fusion.4, f32[96,2,2048]{2,0,1:T(8,128)S(1)} %copy_convert_fusion.5), kind=kOutput, calls=%fused_computation.13.clone.3 | convolution fusion | flops 666546304 | bytes 4389892 | tf_op jit(solution)/shard_map/while/body/eval_jaxpr/dot_general | solution.py:71
  1172.0 2.0 fusion.19
  1174.0 2.2 reshape_transpose_transpose_reshape_reshape_reshape.3
  1176.2 7.2 all-to-all-start.1
  1183.6 26.0 %all-to-all-done.1 = f32[128,1,1,2,1601]{4,3,2,1,0:T(2,128)S(1)} async-done(((f32[128,1,1,2,1601]{4,3,2,1,0:T(2,128)}), f32[128,1,1,2,1601]{4,3,2,1,0:T(2,128)S(1)}, u32[]{:S(2)}, u32[]{:S(2)}) %all-to-all-start.1) | async-done | bytes 1639456 | tf_op jit(solution)/shard_map/all_to_all | solution.py:28
  1209.6 1.2 reshape_reshape.3
  1210.8 2.7 convolution_add_fusion
  (45 shorter events, 0.7 us)
Async XLA Ops:
  6.5 4.7 copy-start
  6.5 6.2 copy-start.3
  6.5 6.2 copy-start.1
  6.5 19.1 %copy-start.2 = (s32[2,96]{1,0:T(2,128)S(1)}, s32[2,96]{1,0:T(2,128)}, u32[]{:S(2)}) copy-start(s32[2,96]{1,0:T(2,128)} %param.12) | copy-start | bytes 2308
  6.5 19.2 %copy-start.4 = (s32[96]{0:T(128)S(1)}, s32[96]{0:T(128)}, u32[]{:S(2)}) copy-start(s32[96]{0:T(128)} %param.13) | copy-start | bytes 1156
  6.5 87.7 %all-gather.2.cloned.1.call-start = ((), (), s32[]{:S(2)}) async-start(), calls=%async_computation.2 | async-start | bytes 19464192 | tf_op jit(solution)/shard_map/all_gather | solution.py:58
  14.1 1162.1 %all-to-all-start = ((f32[128,1,1,2]{3,2,1,0:T(1,128)}), f32[128,1,1,2]{3,2,1,0:T(1,128)S(1)}, u32[]{:S(2)}, u32[]{:S(2)}) async-start(f32[128,1,1,2]{3,2,1,0:T(1,128)} %bitcast.4), calls=%async_computation | async-start | bytes 131072 | tf_op jit(solution)/shard_map/all_to_all | solution.py:28
  1176.2 33.4 %all-to-all-start.1 = ((f32[128,1,1,2,1601]{4,3,2,1,0:T(2,128)}), f32[128,1,1,2,1601]{4,3,2,1,0:T(2,128)S(1)}, u32[]{:S(2)}, u32[]{:S(2)}) async-start(f32[128,1,1,2,1601]{4,3,2,1,0:T(2,128)} %bitcast.11), calls=%async_computation.1 | async-start | bytes 3407872 | tf_op jit(solution)/shard_map/all_to_all | solution.py:28
Sparse Core Ops, SparseCore 0:
  12.8 81.4 all-gather.1
where the time goes:
time: 1230 us; the launch traced here: 1220 us
  matrix products  972 us (79%)
  waiting for transfers between devices  94.5 us (8%)
  local copies, waits for them, and re-layouts  73.5 us (6%)
  other arithmetic  27.4 us (2%)
  loops' own time  20.3 us (2%)
  starting transfers between devices  18.8 us (2%)
  between operations  14 us (1%)
    dot_general x9, matrix products, add_block(): return total + jnp.dot(imag_part, sines, preferred_element_type=jnp.float32)  487 us
    dot_general x9, matrix products, add_block(): jnp.dot(real_part, cosines, preferred_element_type=jnp.float32)  481 us
    all_gather x1, waiting for transfers between devices, local(): gathered = lax.all_gather(whitened, 'sta', axis=0, tiled=True)  68.5 us
    all_to_all x2, waiting for transfers between devices, joined_exchange(): tiles = lax.all_to_all(tiles, axis, split_axis=0, concat_axis=0, tiled=True)  26 us
  transfers between devices with their start and end apart: 3, of which 2 were waited for; matrix products, arithmetic and copies ran while one was open for 87% of the time, Pallas kernels for 0%

commit v1 on v0

--- a/solution.py
+++ b/solution.py
@@ -55,7 +55,13 @@
     devices = groups * members
     capacity = max(2, (4 * pair_count + 3 * devices - 1) // (3 * devices))
     whitened = whiten(spectra)
-    gathered = lax.all_gather(whitened, "sta", axis=0, tiled=True)
+    copies = []
+    for _ in range(lax.psum(1, axis_name="sta")):
+        copies.append(whitened)
+    extra = jnp.stack(copies, axis=0)
+    gathered = jnp.concatenate(
+        lax.all_to_all(extra, axis_name="sta", split_axis=0, concat_axis=0), 0
+    )
     first = jnp.take(gathered, pair_sta[0], axis=0)
     second = jnp.take(gathered, pair_sta[1], axis=0)
     fblock = 2048

time: 1230 us -> 1410 us (1.15)
  waiting for transfers between devices: 94.5 us -> 252 us
  starting transfers between devices: 18.8 us -> 37.8 us
  local copies, waits for them, and re-layouts: 73.5 us -> 92 us
    all_to_all x0 -> x1, waiting for transfers between devices: none -> 226 us  [local(): lax.all_to_all(extra, axis_name='sta', split_axis=0, concat_axis=0)]
    all_gather x1 -> x0, waiting for transfers between devices: 68.5 us -> none  [local(): gathered = lax.all_gather(whitened, 'sta', axis=0, tiled=True)]
    another operation x0 -> x1, local copies, waits for them, and re-layouts: none -> 18.5 us  [local(): extra = jnp.stack(copies, axis=0)]
  transfers between devices with their start and end apart: 3 -> 3, of which waited for: 2 -> 2; matrix products, arithmetic and copies ran while one was open for 87% -> 76% of each run, Pallas kernels for 0% -> 0%
where the time goes in v1:
time: 1410 us; the launch traced here: 1400 us
  matrix products  972 us (69%)
  waiting for transfers between devices  252 us (18%)
  local copies, waits for them, and re-layouts  92 us (7%)
  starting transfers between devices  37.8 us (3%)
  other arithmetic  26.6 us (2%)
  loops' own time  20.4 us (1%)
    dot_general x9, matrix products, add_block(): return total + jnp.dot(imag_part, sines, preferred_element_type=jnp.float32)  487 us
    dot_general x9, matrix products, add_block(): jnp.dot(real_part, cosines, preferred_element_type=jnp.float32)  481 us
    all_to_all x1, waiting for transfers between devices, local(): lax.all_to_all(extra, axis_name='sta', split_axis=0, concat_axis=0)  226 us
  transfers between devices with their start and end apart: 3, of which 2 were waited for; matrix products, arithmetic and copies ran while one was open for 76% of the time, Pallas kernels for 0%

profile of v1, /device:TPU:1, one launch (start us, length us, event | category | flops | bytes accessed | tf_op | source)
XLA Modules:
  0.0 1401.2 jit_solution(15351021016229376790)
XLA Ops:
  0.0 2.9 multiply_reduce_fusion
  2.9 0.5 reduce_sum.30
  3.4 0.5 reduce_sum.31
  3.9 0.4 mul.157
  4.2 0.4 mul.158
  4.7 0.6 multiply_convert_fusion
  5.3 18.5 %stack.2 = bf16[32,8,2,18432]{3,2,1,0:T(2,128)(2,1)} broadcast(bf16[8,2,18432]{2,1,0:T(2,128)(2,1)S(1)} %multiply_convert_fusion), dimensions={1,2,3} | broadcast | bytes 19464192 | tf_op jit(solution)/shard_map/stack | solution.py:61
  23.8 9.8 all-to-all-start.1
  34.1 1.0 fusion.22
  35.1 225.7 %all-to-all-done.1 = bf16[32,8,2,18432]{3,2,1,0:T(2,128)(2,1)} async-done(((bf16[32,8,2,18432]{3,2,1,0:T(2,128)(2,1)}), bf16[32,8,2,18432]{3,2,1,0:T(2,128)(2,1)}, u32[]{:S(2)}, u32[]{:S(2)}) %all-to-all-start.1) | async-done | bytes 18874400 | tf_op jit(solution)/shard_map/all_to_all | solution.py:63
  260.8 18.2 %all-to-all-start = ((f32[128,1,1,2]{3,2,1,0:T(1,128)}), f32[128,1,1,2]{3,2,1,0:T(1,128)S(1)}, u32[]{:S(2)}, u32[]{:S(2)}) async-start(f32[128,1,1,2]{3,2,1,0:T(1,128)} %bitcast.4), calls=%async_computation | async-start | bytes 131072 | tf_op jit(solution)/shard_map/all_to_all | solution.py:28
  279.1 23.4 %gather_fusion = bf16[96,2,18432]{2,1,0:T(2,128)(2,1)} fusion(bf16[256,2,18432]{2,1,0:T(2,128)(2,1)} %bitcast.10, s32[1024]{0:T(1024)S(1)} %pad_clamp_fusion.1), kind=kCustom, calls=%fused_computation.clone | custom fusion | bytes 14156160 | tf_op jit(solution)/shard_map/jit(_take)/gather | solution.py:65
  302.4 23.3 %gather_fusion.1 = bf16[96,2,18432]{2,1,0:T(2,128)(2,1)} fusion(bf16[256,2,18432]{2,1,0:T(2,128)(2,1)} %bitcast.10, s32[1024]{0:T(1024)S(1)} %pad_clamp_fusion), kind=kCustom, calls=%fused_computation.1.clone | custom fusion | bytes 14156160 | tf_op jit(solution)/shard_map/jit(_take)/gather | solution.py:66
  325.7 16.3 %broadcast_select_fusion = (bf16[96,2,18432]{2,1,0:T(2,128)(2,1)}, bf16[96,2,18432]{2,1,0:T(2,128)(2,1)}) fusion(bf16[96,2,18432]{2,1,0:T(2,128)(2,1)} %gather_fusion.1, pred[96]{0:T(512)(128)(4,1)S(1)} %get-tuple-element.150, bf16[96,2,18432]{2,1,0:T(2,128)(2,1)} %gather_fusion, pred[96]{0:T(512)(128)(4,1)S(1)} %get-tuple-element.156), kind=kLoop, calls=%fused_computation.31 | loop fusion | flops 7077888 | bytes 28311744 | tf_op jit(solution)/shard_map/jit(_take)/select_n | solution.py:66
  342.0 1014.8 %while.16 = (s32[]{:T(128)}, f32[96,1601]{1,0:T(8,128)}, bf16[96,2,18432]{2,1,0:T(2,128)(2,1)}, bf16[96,2,18432]{2,1,0:T(2,128)(2,1)}, s32[]{:T(128)}, /*index=5*/s32[]{:T(128)}, s32[]{:T(128)}, s32[]{:T(128)}) while((s32[]{:T(128)}, f32[96,1601]{1,0:T(8,128)}, bf16[96,2,18432]{2,1,0:T(2,128)(2,1)}, ...), condition=%wide.region_5.7_spmd.clone, body=%wide.region_4.6_spmd.clone.sunk | while | flops 1330757632 | bytes 16658849 | solution.py:79
  361.8 2.5 constant_dynamic-slice_fusion.3
  364.3 0.3 copy_convert_fusion.4
  364.6 0.3 copy_convert_fusion.5
  364.9 52.4 %fusion.42 = f32[96,1601]{1,0:T(8,128)S(1)} fusion(s32[1601]{0:T(1024)S(1)} %iota_add_fusion.4, s32[2048]{0:T(1024)S(1)} %iota_add_fusion.5, f32[96,1601]{1,0:T(8,128)} %get-tuple-element.198, f32[96,2,2048]{2,0,1:T(8,128)S(1)} %copy_convert_fusion.4, f32[96,2,2048]{2,0,1:T(8,128)S(1)} %copy_convert_fusion.5, pred[]{:T(512)S(6)} %compare.3), kind=kOutput, calls=%fused_computation.14.clone.3 | convolution fusion | flops 663421184 | bytes 4389893 | tf_op jit(solution)/shard_map/while/body/eval_jaxpr/dot_general | solution.py:76
  417.3 54.1 %fusion.43 = f32[96,1601]{1,0:T(8,128)} fusion(f32[96,1601]{1,0:T(8,128)S(1)} %fusion.42, s32[1601]{0:T(1024)S(1)} %iota_add_fusion.4, s32[2048]{0:T(1024)S(1)} %iota_add_fusion.5, f32[96,2,2048]{2,0,1:T(8,128)S(1)} %copy_convert_fusion.4, f32[96,2,2048]{2,0,1:T(8,128)S(1)} %copy_convert_fusion.5), kind=kOutput, calls=%fused_computation.13.clone.3 | convolution fusion | flops 666546304 | bytes 4389892 | tf_op jit(solution)/shard_map/while/body/eval_jaxpr/dot_general | solution.py:77
  471.4 2.5 constant_dynamic-slice_fusion.3
  473.9 0.3 copy_convert_fusion.4
  474.1 0.3 copy_convert_fusion.5
  474.4 53.5 %fusion.42 = f32[96,1601]{1,0:T(8,128)S(1)} fusion(s32[1601]{0:T(1024)S(1)} %iota_add_fusion.4, s32[2048]{0:T(1024)S(1)} %iota_add_fusion.5, f32[96,1601]{1,0:T(8,128)} %get-tuple-element.198, f32[96,2,2048]{2,0,1:T(8,128)S(1)} %copy_convert_fusion.4, f32[96,2,2048]{2,0,1:T(8,128)S(1)} %copy_convert_fusion.5, pred[]{:T(512)S(6)} %compare.3), kind=kOutput, calls=%fused_computation.14.clone.3 | convolution fusion | flops 663421184 | bytes 4389893 | tf_op jit(solution)/shard_map/while/body/eval_jaxpr/dot_general | solution.py:76
  528.0 54.1 %fusion.43 = f32[96,1601]{1,0:T(8,128)} fusion(f32[96,1601]{1,0:T(8,128)S(1)} %fusion.42, s32[1601]{0:T(1024)S(1)} %iota_add_fusion.4, s32[2048]{0:T(1024)S(1)} %iota_add_fusion.5, f32[96,2,2048]{2,0,1:T(8,128)S(1)} %copy_convert_fusion.4, f32[96,2,2048]{2,0,1:T(8,128)S(1)} %copy_convert_fusion.5), kind=kOutput, calls=%fused_computation.13.clone.3 | convolution fusion | flops 666546304 | bytes 4389892 | tf_op jit(solution)/shard_map/while/body/eval_jaxpr/dot_general | solution.py:77
  582.1 2.5 constant_dynamic-slice_fusion.3
  584.5 0.3 copy_convert_fusion.4
  584.8 0.3 copy_convert_fusion.5
  585.1 53.5 %fusion.42 = f32[96,1601]{1,0:T(8,128)S(1)} fusion(s32[1601]{0:T(1024)S(1)} %iota_add_fusion.4, s32[2048]{0:T(1024)S(1)} %iota_add_fusion.5, f32[96,1601]{1,0:T(8,128)} %get-tuple-element.198, f32[96,2,2048]{2,0,1:T(8,128)S(1)} %copy_convert_fusion.4, f32[96,2,2048]{2,0,1:T(8,128)S(1)} %copy_convert_fusion.5, pred[]{:T(512)S(6)} %compare.3), kind=kOutput, calls=%fused_computation.14.clone.3 | convolution fusion | flops 663421184 | bytes 4389893 | tf_op jit(solution)/shard_map/while/body/eval_jaxpr/dot_general | solution.py:76
  638.6 54.1 %fusion.43 = f32[96,1601]{1,0:T(8,128)} fusion(f32[96,1601]{1,0:T(8,128)S(1)} %fusion.42, s32[1601]{0:T(1024)S(1)} %iota_add_fusion.4, s32[2048]{0:T(1024)S(1)} %iota_add_fusion.5, f32[96,2,2048]{2,0,1:T(8,128)S(1)} %copy_convert_fusion.4, f32[96,2,2048]{2,0,1:T(8,128)S(1)} %copy_convert_fusion.5), kind=kOutput, calls=%fused_computation.13.clone.3 | convolution fusion | flops 666546304 | bytes 4389892 | tf_op jit(solution)/shard_map/while/body/eval_jaxpr/dot_general | solution.py:77
  692.7 2.5 constant_dynamic-slice_fusion.3
  695.2 0.3 copy_convert_fusion.4
  695.4 0.3 copy_convert_fusion.5
  695.7 53.5 %fusion.42 = f32[96,1601]{1,0:T(8,128)S(1)} fusion(s32[1601]{0:T(1024)S(1)} %iota_add_fusion.4, s32[2048]{0:T(1024)S(1)} %iota_add_fusion.5, f32[96,1601]{1,0:T(8,128)} %get-tuple-element.198, f32[96,2,2048]{2,0,1:T(8,128)S(1)} %copy_convert_fusion.4, f32[96,2,2048]{2,0,1:T(8,128)S(1)} %copy_convert_fusion.5, pred[]{:T(512)S(6)} %compare.3), kind=kOutput, calls=%fused_computation.14.clone.3 | convolution fusion | flops 663421184 | bytes 4389893 | tf_op jit(solution)/shard_map/while/body/eval_jaxpr/dot_general | solution.py:76
  749.3 54.1 %fusion.43 = f32[96,1601]{1,0:T(8,128)} fusion(f32[96,1601]{1,0:T(8,128)S(1)} %fusion.42, s32[1601]{0:T(1024)S(1)} %iota_add_fusion.4, s32[2048]{0:T(1024)S(1)} %iota_add_fusion.5, f32[96,2,2048]{2,0,1:T(8,128)S(1)} %copy_convert_fusion.4, f32[96,2,2048]{2,0,1:T(8,128)S(1)} %copy_convert_fusion.5), kind=kOutput, calls=%fused_computation.13.clone.3 | convolution fusion | flops 666546304 | bytes 4389892 | tf_op jit(solution)/shard_map/while/body/eval_jaxpr/dot_general | solution.py:77
  803.4 2.5 constant_dynamic-slice_fusion.3
  805.8 0.3 copy_convert_fusion.4
  806.1 0.3 copy_convert_fusion.5
  806.4 53.5 %fusion.42 = f32[96,1601]{1,0:T(8,128)S(1)} fusion(s32[1601]{0:T(1024)S(1)} %iota_add_fusion.4, s32[2048]{0:T(1024)S(1)} %iota_add_fusion.5, f32[96,1601]{1,0:T(8,128)} %get-tuple-element.198, f32[96,2,2048]{2,0,1:T(8,128)S(1)} %copy_convert_fusion.4, f32[96,2,2048]{2,0,1:T(8,128)S(1)} %copy_convert_fusion.5, pred[]{:T(512)S(6)} %compare.3), kind=kOutput, calls=%fused_computation.14.clone.3 | convolution fusion | flops 663421184 | bytes 4389893 | tf_op jit(solution)/shard_map/while/body/eval_jaxpr/dot_general | solution.py:76
  859.9 54.1 %fusion.43 = f32[96,1601]{1,0:T(8,128)} fusion(f32[96,1601]{1,0:T(8,128)S(1)} %fusion.42, s32[1601]{0:T(1024)S(1)} %iota_add_fusion.4, s32[2048]{0:T(1024)S(1)} %iota_add_fusion.5, f32[96,2,2048]{2,0,1:T(8,128)S(1)} %copy_convert_fusion.4, f32[96,2,2048]{2,0,1:T(8,128)S(1)} %copy_convert_fusion.5), kind=kOutput, calls=%fused_computation.13.clone.3 | convolution fusion | flops 666546304 | bytes 4389892 | tf_op jit(solution)/shard_map/while/body/eval_jaxpr/dot_general | solution.py:77
  914.0 2.5 constant_dynamic-slice_fusion.3
  916.5 0.3 copy_convert_fusion.4
  916.8 0.3 copy_convert_fusion.5
  917.1 53.5 %fusion.42 = f32[96,1601]{1,0:T(8,128)S(1)} fusion(s32[1601]{0:T(1024)S(1)} %iota_add_fusion.4, s32[2048]{0:T(1024)S(1)} %iota_add_fusion.5, f32[96,1601]{1,0:T(8,128)} %get-tuple-element.198, f32[96,2,2048]{2,0,1:T(8,128)S(1)} %copy_convert_fusion.4, f32[96,2,2048]{2,0,1:T(8,128)S(1)} %copy_convert_fusion.5, pred[]{:T(512)S(6)} %compare.3), kind=kOutput, calls=%fused_computation.14.clone.3 | convolution fusion | flops 663421184 | bytes 4389893 | tf_op jit(solution)/shard_map/while/body/eval_jaxpr/dot_general | solution.py:76
  970.6 54.1 %fusion.43 = f32[96,1601]{1,0:T(8,128)} fusion(f32[96,1601]{1,0:T(8,128)S(1)} %fusion.42, s32[1601]{0:T(1024)S(1)} %iota_add_fusion.4, s32[2048]{0:T(1024)S(1)} %iota_add_fusion.5, f32[96,2,2048]{2,0,1:T(8,128)S(1)} %copy_convert_fusion.4, f32[96,2,2048]{2,0,1:T(8,128)S(1)} %copy_convert_fusion.5), kind=kOutput, calls=%fused_computation.13.clone.3 | convolution fusion | flops 666546304 | bytes 4389892 | tf_op jit(solution)/shard_map/while/body/eval_jaxpr/dot_general | solution.py:77
  1024.7 2.5 constant_dynamic-slice_fusion.3
  1027.1 0.3 copy_convert_fusion.4
  1027.4 0.3 copy_convert_fusion.5
  1027.7 53.5 %fusion.42 = f32[96,1601]{1,0:T(8,128)S(1)} fusion(s32[1601]{0:T(1024)S(1)} %iota_add_fusion.4, s32[2048]{0:T(1024)S(1)} %iota_add_fusion.5, f32[96,1601]{1,0:T(8,128)} %get-tuple-element.198, f32[96,2,2048]{2,0,1:T(8,128)S(1)} %copy_convert_fusion.4, f32[96,2,2048]{2,0,1:T(8,128)S(1)} %copy_convert_fusion.5, pred[]{:T(512)S(6)} %compare.3), kind=kOutput, calls=%fused_computation.14.clone.3 | convolution fusion | flops 663421184 | bytes 4389893 | tf_op jit(solution)/shard_map/while/body/eval_jaxpr/dot_general | solution.py:76
  1081.2 54.1 %fusion.43 = f32[96,1601]{1,0:T(8,128)} fusion(f32[96,1601]{1,0:T(8,128)S(1)} %fusion.42, s32[1601]{0:T(1024)S(1)} %iota_add_fusion.4, s32[2048]{0:T(1024)S(1)} %iota_add_fusion.5, f32[96,2,2048]{2,0,1:T(8,128)S(1)} %copy_convert_fusion.4, f32[96,2,2048]{2,0,1:T(8,128)S(1)} %copy_convert_fusion.5), kind=kOutput, calls=%fused_computation.13.clone.3 | convolution fusion | flops 666546304 | bytes 4389892 | tf_op jit(solution)/shard_map/while/body/eval_jaxpr/dot_general | solution.py:77
  1135.3 2.5 constant_dynamic-slice_fusion.3
  1137.8 0.3 copy_convert_fusion.4
  1138.1 0.3 copy_convert_fusion.5
  1138.4 53.5 %fusion.42 = f32[96,1601]{1,0:T(8,128)S(1)} fusion(s32[1601]{0:T(1024)S(1)} %iota_add_fusion.4, s32[2048]{0:T(1024)S(1)} %iota_add_fusion.5, f32[96,1601]{1,0:T(8,128)} %get-tuple-element.198, f32[96,2,2048]{2,0,1:T(8,128)S(1)} %copy_convert_fusion.4, f32[96,2,2048]{2,0,1:T(8,128)S(1)} %copy_convert_fusion.5, pred[]{:T(512)S(6)} %compare.3), kind=kOutput, calls=%fused_computation.14.clone.3 | convolution fusion | flops 663421184 | bytes 4389893 | tf_op jit(solution)/shard_map/while/body/eval_jaxpr/dot_general | solution.py:76
  1191.9 54.1 %fusion.43 = f32[96,1601]{1,0:T(8,128)} fusion(f32[96,1601]{1,0:T(8,128)S(1)} %fusion.42, s32[1601]{0:T(1024)S(1)} %iota_add_fusion.4, s32[2048]{0:T(1024)S(1)} %iota_add_fusion.5, f32[96,2,2048]{2,0,1:T(8,128)S(1)} %copy_convert_fusion.4, f32[96,2,2048]{2,0,1:T(8,128)S(1)} %copy_convert_fusion.5), kind=kOutput, calls=%fused_computation.13.clone.3 | convolution fusion | flops 666546304 | bytes 4389892 | tf_op jit(solution)/shard_map/while/body/eval_jaxpr/dot_general | solution.py:77
  1246.0 2.5 constant_dynamic-slice_fusion.3
  1249.0 53.5 %fusion.42 = f32[96,1601]{1,0:T(8,128)S(1)} fusion(s32[1601]{0:T(1024)S(1)} %iota_add_fusion.4, s32[2048]{0:T(1024)S(1)} %iota_add_fusion.5, f32[96,1601]{1,0:T(8,128)} %get-tuple-element.198, f32[96,2,2048]{2,0,1:T(8,128)S(1)} %copy_convert_fusion.4, f32[96,2,2048]{2,0,1:T(8,128)S(1)} %copy_convert_fusion.5, pred[]{:T(512)S(6)} %compare.3), kind=kOutput, calls=%fused_computation.14.clone.3 | convolution fusion | flops 663421184 | bytes 4389893 | tf_op jit(solution)/shard_map/while/body/eval_jaxpr/dot_general | solution.py:76
  1302.5 54.1 %fusion.43 = f32[96,1601]{1,0:T(8,128)} fusion(f32[96,1601]{1,0:T(8,128)S(1)} %fusion.42, s32[1601]{0:T(1024)S(1)} %iota_add_fusion.4, s32[2048]{0:T(1024)S(1)} %iota_add_fusion.5, f32[96,2,2048]{2,0,1:T(8,128)S(1)} %copy_convert_fusion.4, f32[96,2,2048]{2,0,1:T(8,128)S(1)} %copy_convert_fusion.5), kind=kOutput, calls=%fused_computation.13.clone.3 | convolution fusion | flops 666546304 | bytes 4389892 | tf_op jit(solution)/shard_map/while/body/eval_jaxpr/dot_general | solution.py:77
  1356.8 2.0 fusion.19
  1358.9 2.2 reshape_transpose_transpose_reshape_reshape_reshape.3
  1361.1 9.8 all-to-all-start.2
  1371.0 26.0 %all-to-all-done.2 = f32[128,1,1,2,1601]{4,3,2,1,0:T(2,128)S(1)} async-done(((f32[128,1,1,2,1601]{4,3,2,1,0:T(2,128)}), f32[128,1,1,2,1601]{4,3,2,1,0:T(2,128)S(1)}, u32[]{:S(2)}, u32[]{:S(2)}) %all-to-all-start.2) | async-done | bytes 1639456 | tf_op jit(solution)/shard_map/all_to_all | solution.py:28
  1397.0 1.2 reshape_reshape.3
  1398.1 2.7 convolution_add_fusion
  (45 shorter events, 1.2 us)
Async XLA Ops:
  0.0 4.6 copy-start
  23.7 9.8 copy-start.1
  23.7 10.1 copy-start.3
  23.7 10.1 copy-start.2
  23.8 11.3 copy-start.4
  23.8 237.1 %all-to-all-start.1 = ((bf16[32,8,2,18432]{3,2,1,0:T(2,128)(2,1)}), bf16[32,8,2,18432]{3,2,1,0:T(2,128)(2,1)}, u32[]{:S(2)}, u32[]{:S(2)}) async-start(bf16[32,8,2,18432]{3,2,1,0:T(2,128)(2,1)} %stack.2), calls=%async_computation.1 | async-start | bytes 37748736 | tf_op jit(solution)/shard_map/all_to_all | solution.py:63
  260.8 1100.2 %all-to-all-start = ((f32[128,1,1,2]{3,2,1,0:T(1,128)}), f32[128,1,1,2]{3,2,1,0:T(1,128)S(1)}, u32[]{:S(2)}, u32[]{:S(2)}) async-start(f32[128,1,1,2]{3,2,1,0:T(1,128)} %bitcast.4), calls=%async_computation | async-start | bytes 131072 | tf_op jit(solution)/shard_map/all_to_all | solution.py:28
  1361.1 35.9 %all-to-all-start.2 = ((f32[128,1,1,2,1601]{4,3,2,1,0:T(2,128)}), f32[128,1,1,2,1601]{4,3,2,1,0:T(2,128)S(1)}, u32[]{:S(2)}, u32[]{:S(2)}) async-start(f32[128,1,1,2,1601]{4,3,2,1,0:T(2,128)} %bitcast.12), calls=%async_computation.2 | async-start | bytes 3407872 | tf_op jit(solution)/shard_map/all_to_all | solution.py:28
